TPU v7x, 256 devices: a whole 4x4x8 slice. The times are simulated.
256 devices in a mesh: ctx: 32 (over z, y), head: 8 (over x, core).
Axes of the slice: x: 4, y: 4, z: 8, core: 2. Of those that a mesh axis runs over, the one named last changes fastest.
Arguments:
- queries: bfloat16 [8192, 8192], P('ctx', 'head'), may hold values from -6 to 6
- key_rows: bfloat16 [8192, 1024], P('ctx', 'head'), may hold values from -6 to 6
- value_rows: bfloat16 [8192, 1024], P('ctx', 'head'), may hold values from -6 to 6
- out_grads: bfloat16 [8192, 8192], P(('ctx', 'head')), may hold values from -6 to 6
- doc_ids: int32 [8192], replicated, may hold values from 0 to 7, never falling along the last dimension, each value on 1 to 4096 neighbouring positions
- owner_plan: int32 [32, 32], replicated, may hold values from 0 to 31, each once within a row
Outputs:
- attention: bfloat16 [8192, 8192], P(('ctx', 'head'))
- query_grads: bfloat16 [8192, 8192], P('ctx', 'head')
- key_grads: bfloat16 [8192, 1024], P('ctx', 'head')
- value_grads: bfloat16 [8192, 1024], P('ctx', 'head')
Inputs may be any that keep to these rules, and one draw needn't show every extreme that they name: `owner_plan`: row d lists the owners of the 32 pieces of index d of ctx; each owner once in every row.
All inputs are finite; a program needn't handle non-finite values.
Results may differ from a plain program's by a relative error of at most 0.027.
Values may be sent and summed in bfloat16 or wider, within the bound.
No kernel may reach another device: no remote copies, remote signals or barrier semaphores. Data moves between devices by JAX's collectives and lax.ppermute only.
A program may use at most 64 MiB of HBM per device.

v0:
```python
import jax
import jax.numpy as jnp
from jax import lax
from jax.experimental import pallas as pl
from jax.experimental.pallas import tpu as pltpu
from jax.sharding import Mesh
from jax.sharding import PartitionSpec as P

HD = 128
NZ = 8
NY = 4
TOK = 256
PLANE = NY * TOK
PIECE = 8
DOCLEN = 4096
DOCS = 8
GROUPS = 8
MOST = DOCLEN // PLANE + 1
MASKED = -1e30
LOG2E = 1.4426950408889634
f32 = jnp.float32
bf16 = jnp.bfloat16


def attend_kernel(lo_ref, hi_ref, at_ref, place_ref, start_ref, q_ref, g_ref, *refs):
    own_refs, twin_refs = refs[:NZ], refs[NZ : 2 * NZ]
    refs = refs[2 * NZ :]
    o_ref, dq_ref = refs[:2]
    keep_refs, give_refs = refs[2 : 2 + NZ], refs[2 + NZ : 2 + 2 * NZ]
    kn, vn, dk_acc, dv_acc, s_ref, e_ref = refs[2 + 2 * NZ :]
    rows, width = q_ref.shape
    heads = width // HD
    span = rows // GROUPS
    lanes = span * heads
    scale = HD**-0.5
    half = PLANE // 2
    my_z = at_ref[0]

    for rz in range(NZ):
        z = lax.rem(my_z + NZ - rz, NZ)
        for part, refs_of in ((slice(0, half), own_refs), (slice(half, PLANE), twin_refs)):
            kn[z, part, :] = refs_of[rz][:, :HD]
            vn[z, part, :] = refs_of[rz][:, HD:]

    def gather_heads(ref, at):
        x = ref[at, :]
        return jnp.concatenate([x[:, h * HD : (h + 1) * HD] for h in range(heads)], axis=0)

    def scatter_heads(ref, at, x):
        for h in range(heads):
            ref[at, h * HD : (h + 1) * HD] = x[h * span : (h + 1) * span]

    ones = jnp.ones((8, PLANE), bf16)

    def score(kb, slot, own_plane, qt, place, start, peak):
        s = jnp.dot(kn[kb], qt, preferred_element_type=f32)
        u = lax.broadcasted_iota(jnp.int32, (TOK, lanes), 0)
        for ry in range(NY):
            base = kb * PLANE + at_ref[1 + ry] * TOK
            part = s[ry * TOK : (ry + 1) * TOK]
            seen = u >= start - base
            if own_plane:
                seen = seen & (u <= place - base)
            part = jnp.where(seen, part, MASKED)
            s_ref[slot, ry * TOK : (ry + 1) * TOK, :] = part
            peak = jnp.maximum(peak, jnp.max(part.reshape(TOK // 8, 8, lanes), axis=0))
        return peak

    def weigh(kb, slot, peak, ot, total):
        e = jnp.exp2(s_ref[slot] * (scale * LOG2E) - peak)
        eb = e.astype(bf16)
        e_ref[slot] = eb
        total = total + jnp.dot(ones, eb, preferred_element_type=f32)
        return ot + lax.dot_general(vn[kb], eb, (((0,), (0,)), ((), ())), preferred_element_type=f32), total

    def back(kb, slot, own_plane, gt, delta, qs, gs, dqt):
        dp = jnp.dot(vn[kb], gt, preferred_element_type=f32)
        eb = e_ref[slot]
        ds = (eb.astype(f32) * (dp - delta)).astype(bf16)
        dk = jnp.dot(ds, qs, preferred_element_type=f32)
        dv = jnp.dot(eb, gs, preferred_element_type=f32)
        if own_plane:
            dk_acc[kb] = dk
            dv_acc[kb] = dv
        else:
            dk_acc[kb] += dk
            dv_acc[kb] += dv
        return dqt + lax.dot_general(kn[kb], ds, (((0,), (0,)), ((), ())), preferred_element_type=f32)

    def group(gi, carry):
        at = pl.ds(pl.multiple_of(gi * span, span), span)
        lo = lo_ref[gi]
        place, start = place_ref[gi], start_ref[gi]
        qt = gather_heads(q_ref, at).astype(f32).T
        gt = gather_heads(g_ref, at).astype(f32).T
        qtb, gtb = qt.astype(bf16), gt.astype(bf16)

        peak = score(gi, 0, True, qtb, place, start, jnp.full((8, lanes), MASKED, f32))
        peak = lax.fori_loop(
            lo, gi, lambda kb, x: score(kb, 1 + kb - lo, False, qtb, place, start, x), peak
        )
        peak = jnp.max(peak, axis=0, keepdims=True) * (scale * LOG2E)

        zero = (jnp.zeros((HD, lanes), f32), jnp.zeros((8, lanes), f32))
        ot, total = lax.fori_loop(
            lo, gi, lambda kb, x: weigh(kb, 1 + kb - lo, peak, *x), weigh(gi, 0, peak, *zero)
        )
        inverse = 1.0 / total[:1]
        otb = (ot * inverse).astype(bf16).astype(f32)
        scatter_heads(o_ref, at, otb.T.astype(bf16))
        delta = jnp.sum(otb * gt, axis=0, keepdims=True)
        qs = (qt * inverse).T.astype(bf16)
        gs = (gt * inverse).T.astype(bf16)

        dqt = back(gi, 0, True, gtb, delta, qs, gs, jnp.zeros((HD, lanes), f32))
        dqt = lax.fori_loop(
            lo, gi, lambda kb, x: back(kb, 1 + kb - lo, False, gtb, delta, qs, gs, x), dqt
        )
        scatter_heads(dq_ref, at, (dqt * (inverse * scale)).T.astype(bf16))
        return carry

    lax.fori_loop(0, GROUPS, group, 0)

    for rz in range(NZ):
        z = lax.rem(my_z + rz, NZ)
        for part, refs_of in ((slice(0, half), keep_refs), (slice(half, PLANE), give_refs)):
            refs_of[rz][:, :HD] = (dk_acc[z, part, :] * scale).astype(bf16)
            refs_of[rz][:, HD:] = dv_acc[z, part, :].astype(bf16)


def attend(lo, hi, at, place, start, q, g, own, twin):
    rows, width = q.shape
    lanes = rows // GROUPS * (width // HD)
    vm = pl.BlockSpec(memory_space=pltpu.VMEM)
    sm = pl.BlockSpec(memory_space=pltpu.SMEM)
    outs = (
        [jax.ShapeDtypeStruct((rows, width), bf16)] * 2
        + [jax.ShapeDtypeStruct((PLANE // 2, 2 * HD), bf16)] * (2 * NZ)
    )
    out = pl.pallas_call(
        attend_kernel,
        in_specs=[sm] * 3 + [vm] * (4 + 2 * NZ),
        out_specs=[vm] * len(outs),
        out_shape=outs,
        scratch_shapes=[
            pltpu.VMEM((NZ, PLANE, HD), bf16),
            pltpu.VMEM((NZ, PLANE, HD), bf16),
            pltpu.VMEM((NZ, PLANE, HD), f32),
            pltpu.VMEM((NZ, PLANE, HD), f32),
            pltpu.VMEM((MOST, PLANE, lanes), f32),
            pltpu.VMEM((MOST, PLANE, lanes), bf16),
        ],
        compiler_params=pltpu.CompilerParams(vmem_limit_bytes=52 * 1024 * 1024),
        cost_estimate=pl.CostEstimate(
            flops=12 * 10**9, bytes_accessed=12 * 10**6, transcendentals=4 * 10**6
        ),
        name="attend",
    )(lo, hi, at, place, start, q, g, *own, *twin)
    return out[0], out[1], out[2 : 2 + NZ], out[2 + NZ :]


AXES = ("z", "p", "b", "x", "c")
OWNER = ("z", "p", "c")


def swap(x):
    return lax.ppermute(x, ("b", "c"), [(0, 0), (1, 2), (2, 1), (3, 3)])


def ring(x, step):
    return lax.ppermute(x, "z", [(i, (i + step) % NZ) for i in range(NZ)])


def twin(x):
    return lax.ppermute(x, "c", [(0, 1), (1, 0)])


def swap_across(x):
    pairs = [(4 * p + 2 * b + c, 4 * (1 - p) + 2 * c + b) for p in range(2) for b in range(2) for c in range(2)]
    return lax.ppermute(x, ("p", "b", "c"), pairs)


def nothing(x):
    return x[0, 0].astype(f32) * 0.0


def add(*terms):
    total = terms[0].astype(f32)
    for x in terms[1:]:
        total = total + x.astype(f32)
    return total.astype(bf16)


def body(queries, key_rows, value_rows, out_grads, doc_ids, owner_plan):
    n = NZ * NY
    me = lax.axis_index(OWNER)
    p, c = lax.axis_index("p"), lax.axis_index("c")
    rows, width = queries.shape
    pieces = jnp.arange(n, dtype=jnp.int32)
    owners = lax.dynamic_index_in_dim(owner_plan, me, 0, keepdims=False)

    r = jnp.arange(rows, dtype=jnp.int32)
    owner_row = jnp.repeat(owners, PIECE) * PIECE + r % PIECE
    onehot = (r[:, None] == owner_row[None, :]).astype(bf16)
    outgoing = jnp.dot(onehot, swap(queries), preferred_element_type=f32).astype(bf16)
    q = lax.all_to_all(outgoing.reshape(n, PIECE, width), OWNER, 0, 0, tiled=True).reshape(rows, width)

    mine = jnp.concatenate([key_rows, value_rows], axis=1)
    mine = jnp.concatenate([swap(mine), swap_across(mine)], axis=0)
    g = lax.all_to_all(add(out_grads, nothing(mine)), ("x", "c"), split_axis=1, concat_axis=0, tiled=True)
    g = swap(g)
    ups, downs = [mine], [mine]
    for step in range(NZ // 2):
        ups.append(ring(ups[-1], 1))
        if step < NZ // 2 - 1:
            downs.append(ring(downs[-1], -1))
    own = ups + downs[:0:-1]
    twins = [twin(x) for x in own]

    slot_of = jnp.sum(jnp.where(owner_plan == me, pieces[None, :], 0), axis=1)
    place = (
        pieces[:, None] * TOK + slot_of[:, None] * PIECE + jnp.arange(PIECE, dtype=jnp.int32)[None, :]
    ).reshape(GROUPS, 1, 1, rows // GROUPS)
    docs = jnp.arange(DOCS, dtype=jnp.int32)
    doc_first = jnp.sum((doc_ids[:, None] < docs[None, :]).astype(jnp.int32), axis=0)
    start = jnp.max(jnp.where(doc_first <= place[..., None], doc_first, 0), axis=-1)
    lo = jnp.min(start, axis=(1, 2, 3)) // PLANE
    hi = jnp.max(place, axis=(1, 2, 3)) // PLANE + 1
    spread_lanes = lambda x: jnp.broadcast_to(x, (GROUPS, 1, width // HD, rows // GROUPS)).reshape(GROUPS, 1, -1)
    at = jnp.stack([me // NY] + [2 * (p ^ (j & 1)) + (c ^ (j >> 1)) for j in range(NY)])

    o, dq, keep, give = attend(lo, hi, at, spread_lanes(place), spread_lanes(start), q, g, own, twins)

    returned = lax.all_to_all(dq.reshape(n, PIECE, width), OWNER, 0, 0, tiled=True).reshape(rows, width)
    o = swap(o)
    attention = lax.all_to_all(add(o, nothing(returned)), ("x", "c"), split_axis=0, concat_axis=1, tiled=True)
    query_grads = swap(jnp.dot(onehot.T, returned, preferred_element_type=f32).astype(bf16))

    got = [None] * NZ
    for r in (4, 5, 3, 6, 2, 7, 1, 0):
        got[r] = twin(give[r])
    up = ring(add(keep[4], got[4]), 1)
    down = ring(add(keep[5], got[5]), -1)
    for r in (3, 2, 1):
        up = ring(add(keep[r], got[r], up, *([nothing(o)] if r == 2 else [])), 1)
        if r > 1:
            down = ring(add(keep[9 - r], got[9 - r], down), -1)
    total = add(keep[0], got[0], up, down, nothing(query_grads))
    grads = add(swap(total[:TOK]), swap_across(total[TOK:]))

    return attention, query_grads, grads[:, :HD], grads[:, HD:]


def solution(mesh):
    ctx, head = ("z", "p", "b"), ("x", "c")
    fine = Mesh(mesh.devices.reshape(NZ, 2, 2, -1, 2), AXES)
    rows = P(ctx + head, None)
    return jax.shard_map(
        body,
        mesh=fine,
        in_specs=(P(ctx, head),) * 3 + (rows, P(), P()),
        out_specs=(rows,) + (P(ctx, head),) * 3,
        check_vma=False,
    )
```

profile of v0, /device:TPU:99, one launch (start us, length us, event | category | flops | bytes accessed | tf_op | source)
XLA Modules:
  0.0 165.2 jit_solution(16513393953595034603)
XLA Ops:
  1.6 3.4 %collective-permute-start.3 = (bf16[256,256]{1,0:T(8,128)(2,1)S(1)}, bf16[256,256]{1,0:T(8,128)(2,1)S(1)}, u32[]{:S(2)}, u32[]{:S(2)}) collective-permute-start(bf16[256,256]{1,0:T(8,128)(2,1)S(1)} %constant_dynamic-update-slice_fusion), channel_id=1, source_target_pairs={{0,16},{1,24},{8,17},{9,25},{16,0},{17,8},{24,1},{25,9},{2,18},{3,... | collective-permute-start | bytes 393224 | tf_op jit(solution)/shard_map/ppermute | solution.py:180
  5.0 1.9 %collective-permute-start.1 = (bf16[256,256]{1,0:T(8,128)(2,1)S(1)}, bf16[256,256]{1,0:T(8,128)(2,1)S(1)}, u32[]{:S(2)}, u32[]{:S(2)}) collective-permute-start(bf16[256,256]{1,0:T(8,128)(2,1)S(1)} %constant_dynamic-update-slice_fusion), channel_id=1, source_target_pairs={{0,0},{1,8},{8,1},{9,9},{2,2},{3,10},{10,3},{11,11},{4,4},{5,12},{... | collective-permute-start | bytes 393224 | tf_op jit(solution)/shard_map/ppermute | solution.py:167
  6.9 3.6 %collective-permute-start = (bf16[256,1024]{1,0:T(8,128)(2,1)}, bf16[256,1024]{1,0:T(8,128)(2,1)S(1)}, u32[]{:S(2)}, u32[]{:S(2)}) collective-permute-start(bf16[256,1024]{1,0:T(8,128)(2,1)} %param.6), channel_id=1, source_target_pairs={{0,0},{1,8},{8,1},{9,9},{2,2},{3,10},{10,3},{11,11},{4,4},{5,12},{... | collective-permute-start | bytes 1572872 | tf_op jit(solution)/shard_map/ppermute | solution.py:167
  11.4 2.9 %collective-permute-start.4 = (bf16[512,256]{1,0:T(8,128)(2,1)S(1)}, bf16[512,256]{1,0:T(8,128)(2,1)S(1)}, u32[]{:S(2)}, u32[]{:S(2)}) collective-permute-start(bf16[512,256]{1,0:T(8,128)(2,1)S(1)} %constant_dynamic-update-slice_fusion.2.refs_0_), channel_id=1, source_target_pairs={{0,32},{32,64},{64,96},{96,128},{128,160},{160,192},{192,224},{224... | collective-permute-start | bytes 786440 | tf_op jit(solution)/shard_map/ppermute | solution.py:171
  16.4 4.6 %all-to-all-start.1 = ((bf16[32,8,1024]{2,0,1:T(8,128)(2,1)}), bf16[32,8,1024]{2,0,1:T(8,128)(2,1)S(1)}, u32[]{:S(2)}, u32[]{:S(2)}) async-start(bf16[32,8,1024]{2,0,1:T(8,128)(2,1)} %bitcast.31), calls=%async_computation.1 | async-start | bytes 1048576 | tf_op jit(solution)/shard_map/all_to_all | solution.py:210
  23.7 5.0 %collective-permute-done.5.refs_2_ = bf16[512,256]{1,0:T(8,128)(2,1)S(1)} collective-permute-done((bf16[512,256]{1,0:T(8,128)(2,1)S(1)}, bf16[512,256]{1,0:T(8,128)(2,1)S(1)}, u32[]{:S(2)}, u32[]{:S(2)}) %collective-permute-start.5) | collective-permute-done | bytes 262176 | tf_op jit(solution)/shard_map/ppermute | solution.py:171
  28.8 2.5 %collective-permute-start.6 = (bf16[512,256]{1,0:T(8,128)(2,1)S(1)}, bf16[512,256]{1,0:T(8,128)(2,1)}, u32[]{:S(2)}, u32[]{:S(2)}) collective-permute-start(bf16[512,256]{1,0:T(8,128)(2,1)S(1)} %collective-permute-done.5.refs_2_), channel_id=1, source_target_pairs={{0,32},{32,64},{64,96},{96,128},{128,160},{160,192},{192,224},{224... | collective-permute-start | bytes 786440 | tf_op jit(solution)/shard_map/ppermute | solution.py:171
  32.3 7.7 %all-to-all-start = ((bf16[32,8,1024]{2,1,0:T(8,128)(2,1)}), bf16[32,8,1024]{2,1,0:T(8,128)(2,1)S(1)}, u32[]{:S(2)}, u32[]{:S(2)}) async-start(bf16[32,8,1024]{2,1,0:T(8,128)(2,1)} %fusion), calls=%async_computation | async-start | bytes 1048576 | tf_op jit(solution)/shard_map/all_to_all | solution.py:206
  41.7 2.4 %collective-permute-start.7 = (bf16[512,256]{1,0:T(8,128)(2,1)}, bf16[512,256]{1,0:T(8,128)(2,1)}, u32[]{:S(2)}, u32[]{:S(2)}) collective-permute-start(bf16[512,256]{1,0:T(8,128)(2,1)} %collective-permute-done.6.refs_3_), channel_id=1, source_target_pairs={{0,32},{32,64},{64,96},{96,128},{128,160},{160,192},{192,224},{224... | collective-permute-start | bytes 786440 | tf_op jit(solution)/shard_map/ppermute | solution.py:171
  44.1 2.4 %collective-permute-start.2 = (bf16[256,1024]{1,0:T(8,128)(2,1)S(1)}, bf16[256,1024]{1,0:T(8,128)(2,1)S(1)}, u32[]{:S(2)}, u32[]{:S(2)}) collective-permute-start(bf16[256,1024]{1,0:T(8,128)(2,1)S(1)} %bitcast.35), channel_id=1, source_target_pairs={{0,0},{1,8},{8,1},{9,9},{2,2},{3,10},{10,3},{11,11},{4,4},{5,12},{... | collective-permute-start | bytes 1572872 | tf_op jit(solution)/shard_map/ppermute | solution.py:167
  47.5 12.9 %collective-permute-done.10.refs_5_ = bf16[512,256]{1,0:T(8,128)(2,1)} collective-permute-done((bf16[512,256]{1,0:T(8,128)(2,1)}, bf16[512,256]{1,0:T(8,128)(2,1)}, u32[]{:S(2)}, u32[]{:S(2)}) %collective-permute-start.10) | collective-permute-done | bytes 262176 | tf_op jit(solution)/shard_map/ppermute | solution.py:171
  63.8 31.5 %attend.1 = (bf16[256,1024]{1,0:T(8,128)(2,1)}, bf16[256,1024]{1,0:T(8,128)(2,1)}, bf16[512,256]{1,0:T(8,128)(2,1)S(1)}, bf16[512,256]{1,0:T(8,128)(2,1)S(1)}, b...) custom-call(s32[8]{0:T(128)S(1)} %get-tuple-element.46.lo_ref, ...), custom_call_target="tpu_custom_call" | custom-call | flops 12000000000 | bytes 12000000 | tf_op jit(solution)/shard_map/attend/pallas_call | solution.py:140
  97.6 8.5 %all-to-all-start.2 = ((bf16[32,8,1024]{2,1,0:T(8,128)(2,1)}), bf16[32,8,1024]{2,1,0:T(8,128)(2,1)S(1)}, u32[]{:S(2)}, u32[]{:S(2)}) async-start(bf16[32,8,1024]{2,1,0:T(8,128)(2,1)} %bitcast.11), calls=%async_computation.2 | async-start | bytes 1048576 | tf_op jit(solution)/shard_map/all_to_all | solution.py:234
  106.5 1.9 %collective-permute-start.19 = (bf16[256,1024]{1,0:T(8,128)(2,1)}, bf16[256,1024]{1,0:T(8,128)(2,1)S(1)}, u32[]{:S(2)}, u32[]{:S(2)}) collective-permute-start(bf16[256,1024]{1,0:T(8,128)(2,1)} %get-tuple-element.22), channel_id=1, source_target_pairs={{0,0},{1,8},{8,1},{9,9},{2,2},{3,10},{10,3},{11,11},{4,4},{5,12},{... | collective-permute-start | bytes 1572872 | tf_op jit(solution)/shard_map/ppermute | solution.py:167
  110.5 2.5 %collective-permute-start.27 = (bf16[512,256]{1,0:T(8,128)(2,1)S(1)}, bf16[512,256]{1,0:T(8,128)(2,1)S(1)}, u32[]{:S(2)}, u32[]{:S(2)}) collective-permute-start(bf16[512,256]{1,0:T(8,128)(2,1)S(1)} %add_convert_fusion.8), channel_id=1, source_target_pairs={{0,32},{32,64},{64,96},{96,128},{128,160},{160,192},{192,224},{224... | collective-permute-start | bytes 786440 | tf_op jit(solution)/shard_map/ppermute | solution.py:171
  113.7 12.6 %collective-permute-done.33 = bf16[512,256]{1,0:T(8,128)(2,1)S(1)} collective-permute-done((bf16[512,256]{1,0:T(8,128)(2,1)S(1)}, bf16[512,256]{1,0:T(8,128)(2,1)S(1)}, u32[]{:S(2)}, u32[]{:S(2)}) %collective-permute-start.33) | collective-permute-done | bytes 262176 | tf_op jit(solution)/shard_map/ppermute | solution.py:171
  130.3 2.7 %collective-permute-start.28 = (bf16[512,256]{1,0:T(8,128)(2,1)}, bf16[512,256]{1,0:T(8,128)(2,1)}, u32[]{:S(2)}, u32[]{:S(2)}) collective-permute-start(bf16[512,256]{1,0:T(8,128)(2,1)} %add_convert_fusion.7), channel_id=1, source_target_pairs={{0,32},{32,64},{64,96},{96,128},{128,160},{160,192},{192,224},{224... | collective-permute-start | bytes 786440 | tf_op jit(solution)/shard_map/ppermute | solution.py:171
  133.3 2.9 %collective-permute-start.20 = (bf16[256,1024]{1,0:T(8,128)(2,1)S(1)}, bf16[256,1024]{1,0:T(8,128)(2,1)S(1)}, u32[]{:S(2)}, u32[]{:S(2)}) collective-permute-start(bf16[256,1024]{1,0:T(8,128)(2,1)S(1)} %convolution_convert_fusion), channel_id=1, source_target_pairs={{0,0},{1,8},{8,1},{9,9},{2,2},{3,10},{10,3},{11,11},{4,4},{5,12},{... | collective-permute-start | bytes 1572872 | tf_op jit(solution)/shard_map/ppermute | solution.py:167
  136.2 1.9 %collective-permute-done.34 = bf16[512,256]{1,0:T(8,128)(2,1)} collective-permute-done((bf16[512,256]{1,0:T(8,128)(2,1)S(1)}, bf16[512,256]{1,0:T(8,128)(2,1)}, u32[]{:S(2)}, u32[]{:S(2)}) %collective-permute-start.34) | collective-permute-done | bytes 262176 | tf_op jit(solution)/shard_map/ppermute | solution.py:171
  138.1 1.8 %add_convert_fusion.3 = bf16[512,256]{1,0:T(8,128)(2,1)} fusion(bf16[512,256]{1,0:T(8,128)(2,1)} %collective-permute-done.34, bf16[512,256]{1,0:T(8,128)(2,1)} %collective-permute-done.30, bf16[512,256]{1,0:T(8,128)(2,1)S(1)} %copy-done.2), kind=kLoop, calls=%fused_computation.7 | loop fusion | flops 786432 | bytes 1048576 | tf_op jit(solution)/shard_map/convert_element_type | solution.py:191
  141.8 2.7 %collective-permute-start.29 = (bf16[512,256]{1,0:T(8,128)(2,1)}, bf16[512,256]{1,0:T(8,128)(2,1)}, u32[]{:S(2)}, u32[]{:S(2)}) collective-permute-start(bf16[512,256]{1,0:T(8,128)(2,1)} %add_convert_fusion.6), channel_id=1, source_target_pairs={{0,32},{32,64},{64,96},{96,128},{128,160},{160,192},{192,224},{224... | collective-permute-start | bytes 786440 | tf_op jit(solution)/shard_map/ppermute | solution.py:171
  146.5 6.4 %all-to-all-start.3 = ((bf16[8,32,1024]{2,1,0:T(8,128)(2,1)}), bf16[8,32,1024]{2,1,0:T(8,128)(2,1)S(1)}, u32[]{:S(2)}, u32[]{:S(2)}) async-start(bf16[8,32,1024]{2,1,0:T(8,128)(2,1)} %bitcast.14), calls=%async_computation.3 | async-start | bytes 1048576 | tf_op jit(solution)/shard_map/all_to_all | solution.py:236
  155.3 2.1 %collective-permute-start.36 = (bf16[256,256]{1,0:T(8,128)(2,1)S(1)}, bf16[256,256]{1,0:T(8,128)(2,1)S(1)}, u32[]{:S(2)}, u32[]{:S(2)}) collective-permute-start(bf16[256,256]{1,0:T(8,128)(2,1)S(1)} %get-tuple-element.40), channel_id=1, source_target_pairs={{0,0},{1,8},{8,1},{9,9},{2,2},{3,10},{10,3},{11,11},{4,4},{5,12},{... | collective-permute-start | bytes 393224 | tf_op jit(solution)/shard_map/ppermute | solution.py:167
  157.4 3.1 %collective-permute-start.37 = (bf16[256,256]{1,0:T(8,128)(2,1)S(1)}, bf16[256,256]{1,0:T(8,128)(2,1)S(1)}, u32[]{:S(2)}, u32[]{:S(2)}) collective-permute-start(bf16[256,256]{1,0:T(8,128)(2,1)S(1)} %get-tuple-element.41), channel_id=1, source_target_pairs={{0,16},{1,24},{8,17},{9,25},{16,0},{17,8},{24,1},{25,9},{2,18},{3,... | collective-permute-start | bytes 393224 | tf_op jit(solution)/shard_map/ppermute | solution.py:180
  (147 shorter events, 31.5 us)
Async XLA Ops:
  6.9 24.3 %collective-permute-start = (bf16[256,1024]{1,0:T(8,128)(2,1)}, bf16[256,1024]{1,0:T(8,128)(2,1)S(1)}, u32[]{:S(2)}, u32[]{:S(2)}) collective-permute-start(bf16[256,1024]{1,0:T(8,128)(2,1)} %param.6), channel_id=1, source_target_pairs={{0,0},{1,8},{8,1},{9,9},{2,2},{3,10},{10,3},{11,11},{4,4},{5,12},{... | collective-permute-start | bytes 1572872 | tf_op jit(solution)/shard_map/ppermute | solution.py:167
  16.4 15.9 %all-to-all-start.1 = ((bf16[32,8,1024]{2,0,1:T(8,128)(2,1)}), bf16[32,8,1024]{2,0,1:T(8,128)(2,1)S(1)}, u32[]{:S(2)}, u32[]{:S(2)}) async-start(bf16[32,8,1024]{2,0,1:T(8,128)(2,1)} %bitcast.31), calls=%async_computation.1 | async-start | bytes 1048576 | tf_op jit(solution)/shard_map/all_to_all | solution.py:210
  22.8 18.2 %collective-permute-start.11 = (bf16[512,256]{1,0:T(8,128)(2,1)S(1)}, bf16[512,256]{1,0:T(8,128)(2,1)S(1)}, u32[]{:S(2)}, u32[]{:S(2)}) collective-permute-start(bf16[512,256]{1,0:T(8,128)(2,1)S(1)} %constant_dynamic-update-slice_fusion.2.refs_0_), channel_id=1, source_target_pairs={{0,1},{1,0},{2,3},{3,2},{4,5},{5,4},{6,7},{7,6},{8,9},{9,8},{10,11... | collective-permute-start | bytes 786440 | tf_op jit(solution)/shard_map/ppermute | solution.py:175
  23.5 20.6 %collective-permute-start.18 = (bf16[512,256]{1,0:T(8,128)(2,1)S(1)}, bf16[512,256]{1,0:T(8,128)(2,1)S(1)}, u32[]{:S(2)}, u32[]{:S(2)}) collective-permute-start(bf16[512,256]{1,0:T(8,128)(2,1)S(1)} %collective-permute-done.8.refs_7_), channel_id=1, source_target_pairs={{0,1},{1,0},{2,3},{3,2},{4,5},{5,4},{6,7},{7,6},{8,9},{9,8},{10,11... | collective-permute-start | bytes 786440 | tf_op jit(solution)/shard_map/ppermute | solution.py:175
  23.6 17.2 %collective-permute-start.9 = (bf16[512,256]{1,0:T(8,128)(2,1)S(1)}, bf16[512,256]{1,0:T(8,128)(2,1)}, u32[]{:S(2)}, u32[]{:S(2)}) collective-permute-start(bf16[512,256]{1,0:T(8,128)(2,1)S(1)} %collective-permute-done.8.refs_7_), channel_id=1, source_target_pairs={{0,224},{32,0},{64,32},{96,64},{128,96},{160,128},{192,160},{224,1... | collective-permute-start | bytes 786440 | tf_op jit(solution)/shard_map/ppermute | solution.py:171
  28.8 12.5 %collective-permute-start.6 = (bf16[512,256]{1,0:T(8,128)(2,1)S(1)}, bf16[512,256]{1,0:T(8,128)(2,1)}, u32[]{:S(2)}, u32[]{:S(2)}) collective-permute-start(bf16[512,256]{1,0:T(8,128)(2,1)S(1)} %collective-permute-done.5.refs_2_), channel_id=1, source_target_pairs={{0,32},{32,64},{64,96},{96,128},{128,160},{160,192},{192,224},{224... | collective-permute-start | bytes 786440 | tf_op jit(solution)/shard_map/ppermute | solution.py:171
  32.3 30.7 %all-to-all-start = ((bf16[32,8,1024]{2,1,0:T(8,128)(2,1)}), bf16[32,8,1024]{2,1,0:T(8,128)(2,1)S(1)}, u32[]{:S(2)}, u32[]{:S(2)}) async-start(bf16[32,8,1024]{2,1,0:T(8,128)(2,1)} %fusion), calls=%async_computation | async-start | bytes 1048576 | tf_op jit(solution)/shard_map/all_to_all | solution.py:206
  40.9 19.4 %collective-permute-start.10 = (bf16[512,256]{1,0:T(8,128)(2,1)}, bf16[512,256]{1,0:T(8,128)(2,1)}, u32[]{:S(2)}, u32[]{:S(2)}) collective-permute-start(bf16[512,256]{1,0:T(8,128)(2,1)} %collective-permute-done.9.refs_6_), channel_id=1, source_target_pairs={{0,224},{32,0},{64,32},{96,64},{128,96},{160,128},{192,160},{224,1... | collective-permute-start | bytes 786440 | tf_op jit(solution)/shard_map/ppermute | solution.py:171
  41.7 19.5 %collective-permute-start.7 = (bf16[512,256]{1,0:T(8,128)(2,1)}, bf16[512,256]{1,0:T(8,128)(2,1)}, u32[]{:S(2)}, u32[]{:S(2)}) collective-permute-start(bf16[512,256]{1,0:T(8,128)(2,1)} %collective-permute-done.6.refs_3_), channel_id=1, source_target_pairs={{0,32},{32,64},{64,96},{96,128},{128,160},{160,192},{192,224},{224... | collective-permute-start | bytes 786440 | tf_op jit(solution)/shard_map/ppermute | solution.py:171
  44.1 17.6 %collective-permute-start.2 = (bf16[256,1024]{1,0:T(8,128)(2,1)S(1)}, bf16[256,1024]{1,0:T(8,128)(2,1)S(1)}, u32[]{:S(2)}, u32[]{:S(2)}) collective-permute-start(bf16[256,1024]{1,0:T(8,128)(2,1)S(1)} %bitcast.35), channel_id=1, source_target_pairs={{0,0},{1,8},{8,1},{9,9},{2,2},{3,10},{10,3},{11,11},{4,4},{5,12},{... | collective-permute-start | bytes 1572872 | tf_op jit(solution)/shard_map/ppermute | solution.py:167
  46.9 14.9 %collective-permute-start.13 = (bf16[512,256]{1,0:T(8,128)(2,1)S(1)}, bf16[512,256]{1,0:T(8,128)(2,1)S(1)}, u32[]{:S(2)}, u32[]{:S(2)}) collective-permute-start(bf16[512,256]{1,0:T(8,128)(2,1)S(1)} %collective-permute-done.5.refs_2_), channel_id=1, source_target_pairs={{0,1},{1,0},{2,3},{3,2},{4,5},{5,4},{6,7},{7,6},{8,9},{9,8},{10,11... | collective-permute-start | bytes 786440 | tf_op jit(solution)/shard_map/ppermute | solution.py:175
  47.0 15.7 %collective-permute-start.14 = (bf16[512,256]{1,0:T(8,128)(2,1)}, bf16[512,256]{1,0:T(8,128)(2,1)S(1)}, u32[]{:S(2)}, u32[]{:S(2)}) collective-permute-start(bf16[512,256]{1,0:T(8,128)(2,1)} %collective-permute-done.6.refs_3_), channel_id=1, source_target_pairs={{0,1},{1,0},{2,3},{3,2},{4,5},{5,4},{6,7},{7,6},{8,9},{9,8},{10,11... | collective-permute-start | bytes 786440 | tf_op jit(solution)/shard_map/ppermute | solution.py:175
  95.8 12.7 %collective-permute-start.32 = (bf16[512,256]{1,0:T(8,128)(2,1)}, bf16[512,256]{1,0:T(8,128)(2,1)S(1)}, u32[]{:S(2)}, u32[]{:S(2)}) collective-permute-start(bf16[512,256]{1,0:T(8,128)(2,1)} %get-tuple-element.39), channel_id=1, source_target_pairs={{0,1},{1,0},{2,3},{3,2},{4,5},{5,4},{6,7},{7,6},{8,9},{9,8},{10,11... | collective-permute-start | bytes 786440 | tf_op jit(solution)/shard_map/ppermute | solution.py:175
  95.9 13.0 %collective-permute-start.24 = (bf16[512,256]{1,0:T(8,128)(2,1)}, bf16[512,256]{1,0:T(8,128)(2,1)S(1)}, u32[]{:S(2)}, u32[]{:S(2)}) collective-permute-start(bf16[512,256]{1,0:T(8,128)(2,1)} %get-tuple-element.31), channel_id=1, source_target_pairs={{0,1},{1,0},{2,3},{3,2},{4,5},{5,4},{6,7},{7,6},{8,9},{9,8},{10,11... | collective-permute-start | bytes 786440 | tf_op jit(solution)/shard_map/ppermute | solution.py:175
  97.6 35.4 %all-to-all-start.2 = ((bf16[32,8,1024]{2,1,0:T(8,128)(2,1)}), bf16[32,8,1024]{2,1,0:T(8,128)(2,1)S(1)}, u32[]{:S(2)}, u32[]{:S(2)}) async-start(bf16[32,8,1024]{2,1,0:T(8,128)(2,1)} %bitcast.11), calls=%async_computation.2 | async-start | bytes 1048576 | tf_op jit(solution)/shard_map/all_to_all | solution.py:234
  106.5 20.7 %collective-permute-start.19 = (bf16[256,1024]{1,0:T(8,128)(2,1)}, bf16[256,1024]{1,0:T(8,128)(2,1)S(1)}, u32[]{:S(2)}, u32[]{:S(2)}) collective-permute-start(bf16[256,1024]{1,0:T(8,128)(2,1)} %get-tuple-element.22), channel_id=1, source_target_pairs={{0,0},{1,8},{8,1},{9,9},{2,2},{3,10},{10,3},{11,11},{4,4},{5,12},{... | collective-permute-start | bytes 1572872 | tf_op jit(solution)/shard_map/ppermute | solution.py:167
  108.5 17.8 %collective-permute-start.33 = (bf16[512,256]{1,0:T(8,128)(2,1)S(1)}, bf16[512,256]{1,0:T(8,128)(2,1)S(1)}, u32[]{:S(2)}, u32[]{:S(2)}) collective-permute-start(bf16[512,256]{1,0:T(8,128)(2,1)S(1)} %add_convert_fusion.5), channel_id=1, source_target_pairs={{0,224},{32,0},{64,32},{96,64},{128,96},{160,128},{192,160},{224,1... | collective-permute-start | bytes 786440 | tf_op jit(solution)/shard_map/ppermute | solution.py:171
  109.4 19.8 %collective-permute-start.23 = (bf16[512,256]{1,0:T(8,128)(2,1)S(1)}, bf16[512,256]{1,0:T(8,128)(2,1)S(1)}, u32[]{:S(2)}, u32[]{:S(2)}) collective-permute-start(bf16[512,256]{1,0:T(8,128)(2,1)S(1)} %copy-done.16), channel_id=1, source_target_pairs={{0,1},{1,0},{2,3},{3,2},{4,5},{5,4},{6,7},{7,6},{8,9},{9,8},{10,11... | collective-permute-start | bytes 786440 | tf_op jit(solution)/shard_map/ppermute | solution.py:175
  110.5 19.0 %collective-permute-start.27 = (bf16[512,256]{1,0:T(8,128)(2,1)S(1)}, bf16[512,256]{1,0:T(8,128)(2,1)S(1)}, u32[]{:S(2)}, u32[]{:S(2)}) collective-permute-start(bf16[512,256]{1,0:T(8,128)(2,1)S(1)} %add_convert_fusion.8), channel_id=1, source_target_pairs={{0,32},{32,64},{64,96},{96,128},{128,160},{160,192},{192,224},{224... | collective-permute-start | bytes 786440 | tf_op jit(solution)/shard_map/ppermute | solution.py:171
  112.9 41.2 %collective-permute-start.21 = (bf16[512,256]{1,0:T(8,128)(2,1)}, bf16[512,256]{1,0:T(8,128)(2,1)S(1)}, u32[]{:S(2)}, u32[]{:S(2)}) collective-permute-start(bf16[512,256]{1,0:T(8,128)(2,1)} %get-tuple-element.25), channel_id=1, source_target_pairs={{0,1},{1,0},{2,3},{3,2},{4,5},{5,4},{6,7},{7,6},{8,9},{9,8},{10,11... | collective-permute-start | bytes 786440 | tf_op jit(solution)/shard_map/ppermute | solution.py:175
  126.3 13.7 %collective-permute-start.22 = (bf16[512,256]{1,0:T(8,128)(2,1)}, bf16[512,256]{1,0:T(8,128)(2,1)}, u32[]{:S(2)}, u32[]{:S(2)}) collective-permute-start(bf16[512,256]{1,0:T(8,128)(2,1)} %get-tuple-element.27), channel_id=1, source_target_pairs={{0,1},{1,0},{2,3},{3,2},{4,5},{5,4},{6,7},{7,6},{8,9},{9,8},{10,11... | collective-permute-start | bytes 786440 | tf_op jit(solution)/shard_map/ppermute | solution.py:175
  133.3 19.6 %collective-permute-start.20 = (bf16[256,1024]{1,0:T(8,128)(2,1)S(1)}, bf16[256,1024]{1,0:T(8,128)(2,1)S(1)}, u32[]{:S(2)}, u32[]{:S(2)}) collective-permute-start(bf16[256,1024]{1,0:T(8,128)(2,1)S(1)} %convolution_convert_fusion), channel_id=1, source_target_pairs={{0,0},{1,8},{8,1},{9,9},{2,2},{3,10},{10,3},{11,11},{4,4},{5,12},{... | collective-permute-start | bytes 1572872 | tf_op jit(solution)/shard_map/ppermute | solution.py:167
  140.0 14.2 %collective-permute-start.35 = (bf16[512,256]{1,0:T(8,128)(2,1)}, bf16[512,256]{1,0:T(8,128)(2,1)S(1)}, u32[]{:S(2)}, u32[]{:S(2)}) collective-permute-start(bf16[512,256]{1,0:T(8,128)(2,1)} %add_convert_fusion.3), channel_id=1, source_target_pairs={{0,224},{32,0},{64,32},{96,64},{128,96},{160,128},{192,160},{224,1... | collective-permute-start | bytes 786440 | tf_op jit(solution)/shard_map/ppermute | solution.py:171
  146.5 14.8 %all-to-all-start.3 = ((bf16[8,32,1024]{2,1,0:T(8,128)(2,1)}), bf16[8,32,1024]{2,1,0:T(8,128)(2,1)S(1)}, u32[]{:S(2)}, u32[]{:S(2)}) async-start(bf16[8,32,1024]{2,1,0:T(8,128)(2,1)} %bitcast.14), calls=%async_computation.3 | async-start | bytes 1048576 | tf_op jit(solution)/shard_map/all_to_all | solution.py:236
  (35 other events, 256.4 us)
where the time goes:
time: 168 us; the launch traced here: 165 us
  starting transfers between devices  72.7 us (43%)
  waiting for transfers between devices  37.5 us (22%)
  Pallas kernels  31.5 us (19%)
  local copies, waits for them, and re-layouts  9.63 us (6%)
  other arithmetic  8.62 us (5%)
  between operations  3.79 us (2%)
    ppermute x14, waiting for transfers between devices, ring(): return lax.ppermute(x, 'z', [(i, (i + step) % NZ) for i in range(NZ)])  32.5 us
    pallas_call x1, Pallas kernels, attend(): pl.pallas_call(attend_kernel, in_specs=[sm] * 3 + [vm] * (4 + 2 * NZ), ou...  31.5 us
    ppermute x14, starting transfers between devices, ring(): return lax.ppermute(x, 'z', [(i, (i + step) % NZ) for i in range(NZ)])  18.6 us
    ppermute x6, starting transfers between devices, swap(): return lax.ppermute(x, ('b', 'c'), [(0, 0), (1, 2), (2, 1), (3, 3)])  14.9 us
    all_to_all x1, starting transfers between devices, body(): lax.all_to_all(dq.reshape(n, PIECE, width), OWNER, 0, 0, tiled=True)  8.45 us
    convert_element_type x11, other arithmetic, add(): return total.astype(bf16)  7.89 us
    all_to_all x1, starting transfers between devices, body(): lax.all_to_all(outgoing.reshape(n, PIECE, width), OWNER, 0, 0, tiled=True)  7.68 us
    ppermute x2, starting transfers between devices, swap_across(): return lax.ppermute(x, ('p', 'b', 'c'), pairs)  6.5 us
  transfers between devices with their start and end apart: 42, of which 11 were waited for; matrix products, arithmetic and copies ran while one was open for 9% of the time, Pallas kernels for 0%

commit v1 on v0

--- a/solution.py
+++ b/solution.py
@@ -242,13 +242,14 @@
     up = ring(add(keep[4], got[4]), 1)
     down = ring(add(keep[5], got[5]), -1)
     for r in (3, 2, 1):
-        up = ring(add(keep[r], got[r], up, *([nothing(o)] if r == 2 else [])), 1)
+        up = ring(add(keep[r], got[r], up, *([nothing(o), nothing(returned)] if r == 1 else [])), 1)
         if r > 1:
             down = ring(add(keep[9 - r], got[9 - r], down), -1)
-    total = add(keep[0], got[0], up, down, nothing(query_grads))
-    grads = add(swap(total[:TOK]), swap_across(total[TOK:]))
-
-    return attention, query_grads, grads[:, :HD], grads[:, HD:]
+    total = add(keep[0], got[0], up, down)
+    near, far = swap(total[:TOK]), swap_across(total[TOK:])
+    key_grads, value_grads = (add(near[:, cols], far[:, cols]) for cols in (slice(0, HD), slice(HD, 2 * HD)))
+
+    return attention, query_grads, key_grads, value_grads
 
 
 def solution(mesh):

time: 168 us -> 167 us (level); the launches traced: 165 us -> 167 us
  Pallas kernels: 31.5 us -> 36.7 us
  other arithmetic: 8.62 us -> 4.61 us
  waiting for transfers between devices: 37.5 us -> 40.8 us
  local copies, waits for them, and re-layouts: 9.63 us -> 7.23 us
    pallas_call x1, Pallas kernels: 31.5 us -> 36.7 us  [attend(): pl.pallas_call(attend_kernel, in_specs=[sm] * 3 + [vm] * (4 + 2 * NZ), ou...]
    convert_element_type x11, other arithmetic: 7.89 us -> 3.89 us  [add(): return total.astype(bf16)]
    ppermute x14, waiting for transfers between devices: 32.5 us -> 35 us  [ring(): return lax.ppermute(x, 'z', [(i, (i + step) % NZ) for i in range(NZ)])]
    all_to_all x1, starting transfers between devices: 6.4 us -> 4.56 us  [body(): lax.all_to_all(add(o, nothing(returned)), ('x', 'c'), split_axis=0, conca...]
    unnamed x37 -> x39, local copies, waits for them, and re-layouts: 4.3 us -> 3.07 us
  transfers between devices with their start and end apart: 42 -> 42, of which waited for: 11 -> 10; matrix products, arithmetic and copies ran while one was open for 9% -> 6% of each run, Pallas kernels for 0% -> 0%
where the time goes in v1:
time: 167 us
  starting transfers between devices  72.7 us (44%)
  waiting for transfers between devices  40.8 us (24%)
  Pallas kernels  36.7 us (22%)
  local copies, waits for them, and re-layouts  7.23 us (4%)
  other arithmetic  4.61 us (3%)
  between operations  3.15 us (2%)
    pallas_call x1, Pallas kernels, attend(): pl.pallas_call(attend_kernel, in_specs=[sm] * 3 + [vm] * (4 + 2 * NZ), ou...  36.7 us
    ppermute x14, waiting for transfers between devices, ring(): return lax.ppermute(x, 'z', [(i, (i + step) % NZ) for i in range(NZ)])  35 us
    ppermute x14, starting transfers between devices, ring(): return lax.ppermute(x, 'z', [(i, (i + step) % NZ) for i in range(NZ)])  18.4 us
    ppermute x6, starting transfers between devices, swap(): return lax.ppermute(x, ('b', 'c'), [(0, 0), (1, 2), (2, 1), (3, 3)])  16.5 us
    all_to_all x1, starting transfers between devices, body(): lax.all_to_all(dq.reshape(n, PIECE, width), OWNER, 0, 0, tiled=True)  8.43 us
    all_to_all x1, starting transfers between devices, body(): lax.all_to_all(outgoing.reshape(n, PIECE, width), OWNER, 0, 0, tiled=True)  7.67 us
    ppermute x2, starting transfers between devices, swap_across(): return lax.ppermute(x, ('p', 'b', 'c'), pairs)  7.21 us
    ppermute x16, starting transfers between devices, twin(): return lax.ppermute(x, 'c', [(0, 1), (1, 0)])  5.34 us
  transfers between devices with their start and end apart: 42, of which 10 were waited for; matrix products, arithmetic and copies ran while one was open for 6% of the time, Pallas kernels for 0%

profile of v1, /device:TPU:99, one launch (start us, length us, event | category | flops | bytes accessed | tf_op | source)
XLA Modules:
  0.0 166.6 jit_solution(782816545500828518)
XLA Ops:
  1.6 3.4 %collective-permute-start.3 = (bf16[256,256]{1,0:T(8,128)(2,1)S(1)}, bf16[256,256]{1,0:T(8,128)(2,1)S(1)}, u32[]{:S(2)}, u32[]{:S(2)}) collective-permute-start(bf16[256,256]{1,0:T(8,128)(2,1)S(1)} %constant_dynamic-update-slice_fusion), channel_id=1, source_target_pairs={{0,16},{1,24},{8,17},{9,25},{16,0},{17,8},{24,1},{25,9},{2,18},{3,... | collective-permute-start | bytes 393224 | tf_op jit(solution)/shard_map/ppermute | solution.py:180
  5.0 1.9 %collective-permute-start.1 = (bf16[256,256]{1,0:T(8,128)(2,1)S(1)}, bf16[256,256]{1,0:T(8,128)(2,1)S(1)}, u32[]{:S(2)}, u32[]{:S(2)}) collective-permute-start(bf16[256,256]{1,0:T(8,128)(2,1)S(1)} %constant_dynamic-update-slice_fusion), channel_id=1, source_target_pairs={{0,0},{1,8},{8,1},{9,9},{2,2},{3,10},{10,3},{11,11},{4,4},{5,12},{... | collective-permute-start | bytes 393224 | tf_op jit(solution)/shard_map/ppermute | solution.py:167
  6.9 3.6 %collective-permute-start = (bf16[256,1024]{1,0:T(8,128)(2,1)}, bf16[256,1024]{1,0:T(8,128)(2,1)S(1)}, u32[]{:S(2)}, u32[]{:S(2)}) collective-permute-start(bf16[256,1024]{1,0:T(8,128)(2,1)} %param.6), channel_id=1, source_target_pairs={{0,0},{1,8},{8,1},{9,9},{2,2},{3,10},{10,3},{11,11},{4,4},{5,12},{... | collective-permute-start | bytes 1572872 | tf_op jit(solution)/shard_map/ppermute | solution.py:167
  11.4 2.9 %collective-permute-start.4 = (bf16[512,256]{1,0:T(8,128)(2,1)S(1)}, bf16[512,256]{1,0:T(8,128)(2,1)S(1)}, u32[]{:S(2)}, u32[]{:S(2)}) collective-permute-start(bf16[512,256]{1,0:T(8,128)(2,1)S(1)} %constant_dynamic-update-slice_fusion.2.refs_0_), channel_id=1, source_target_pairs={{0,32},{32,64},{64,96},{96,128},{128,160},{160,192},{192,224},{224... | collective-permute-start | bytes 786440 | tf_op jit(solution)/shard_map/ppermute | solution.py:171
  16.4 4.6 %all-to-all-start.1 = ((bf16[32,8,1024]{2,0,1:T(8,128)(2,1)}), bf16[32,8,1024]{2,0,1:T(8,128)(2,1)S(1)}, u32[]{:S(2)}, u32[]{:S(2)}) async-start(bf16[32,8,1024]{2,0,1:T(8,128)(2,1)} %bitcast.30), calls=%async_computation.1 | async-start | bytes 1048576 | tf_op jit(solution)/shard_map/all_to_all | solution.py:210
  23.7 5.0 %collective-permute-done.5.refs_2_ = bf16[512,256]{1,0:T(8,128)(2,1)S(1)} collective-permute-done((bf16[512,256]{1,0:T(8,128)(2,1)S(1)}, bf16[512,256]{1,0:T(8,128)(2,1)S(1)}, u32[]{:S(2)}, u32[]{:S(2)}) %collective-permute-start.5) | collective-permute-done | bytes 262176 | tf_op jit(solution)/shard_map/ppermute | solution.py:171
  28.8 2.5 %collective-permute-start.6 = (bf16[512,256]{1,0:T(8,128)(2,1)S(1)}, bf16[512,256]{1,0:T(8,128)(2,1)}, u32[]{:S(2)}, u32[]{:S(2)}) collective-permute-start(bf16[512,256]{1,0:T(8,128)(2,1)S(1)} %collective-permute-done.5.refs_2_), channel_id=1, source_target_pairs={{0,32},{32,64},{64,96},{96,128},{128,160},{160,192},{192,224},{224... | collective-permute-start | bytes 786440 | tf_op jit(solution)/shard_map/ppermute | solution.py:171
  32.4 7.7 %all-to-all-start = ((bf16[32,8,1024]{2,1,0:T(8,128)(2,1)}), bf16[32,8,1024]{2,1,0:T(8,128)(2,1)S(1)}, u32[]{:S(2)}, u32[]{:S(2)}) async-start(bf16[32,8,1024]{2,1,0:T(8,128)(2,1)} %fusion), calls=%async_computation | async-start | bytes 1048576 | tf_op jit(solution)/shard_map/all_to_all | solution.py:206
  41.2 2.4 %collective-permute-start.7 = (bf16[512,256]{1,0:T(8,128)(2,1)}, bf16[512,256]{1,0:T(8,128)(2,1)}, u32[]{:S(2)}, u32[]{:S(2)}) collective-permute-start(bf16[512,256]{1,0:T(8,128)(2,1)} %collective-permute-done.6.refs_3_), channel_id=1, source_target_pairs={{0,32},{32,64},{64,96},{96,128},{128,160},{160,192},{192,224},{224... | collective-permute-start | bytes 786440 | tf_op jit(solution)/shard_map/ppermute | solution.py:171
  43.7 2.7 %collective-permute-start.2 = (bf16[256,1024]{1,0:T(8,128)(2,1)S(1)}, bf16[256,1024]{1,0:T(8,128)(2,1)S(1)}, u32[]{:S(2)}, u32[]{:S(2)}) collective-permute-start(bf16[256,1024]{1,0:T(8,128)(2,1)S(1)} %bitcast.34), channel_id=1, source_target_pairs={{0,0},{1,8},{8,1},{9,9},{2,2},{3,10},{10,3},{11,11},{4,4},{5,12},{... | collective-permute-start | bytes 1572872 | tf_op jit(solution)/shard_map/ppermute | solution.py:167
  47.3 13.0 %collective-permute-done.10.refs_5_ = bf16[512,256]{1,0:T(8,128)(2,1)} collective-permute-done((bf16[512,256]{1,0:T(8,128)(2,1)}, bf16[512,256]{1,0:T(8,128)(2,1)}, u32[]{:S(2)}, u32[]{:S(2)}) %collective-permute-start.10) | collective-permute-done | bytes 262176 | tf_op jit(solution)/shard_map/ppermute | solution.py:171
  63.8 36.7 %attend.1 = (bf16[256,1024]{1,0:T(8,128)(2,1)}, bf16[256,1024]{1,0:T(8,128)(2,1)}, bf16[512,256]{1,0:T(8,128)(2,1)S(1)}, bf16[512,256]{1,0:T(8,128)(2,1)S(1)}, b...) custom-call(s32[8]{0:T(128)S(1)} %get-tuple-element.46.lo_ref, ...), custom_call_target="tpu_custom_call" | custom-call | flops 12000000000 | bytes 12000000 | tf_op jit(solution)/shard_map/attend/pallas_call | solution.py:140
  102.8 8.4 %all-to-all-start.2 = ((bf16[32,8,1024]{2,1,0:T(8,128)(2,1)}), bf16[32,8,1024]{2,1,0:T(8,128)(2,1)S(1)}, u32[]{:S(2)}, u32[]{:S(2)}) async-start(bf16[32,8,1024]{2,1,0:T(8,128)(2,1)} %bitcast.11), calls=%async_computation.2 | async-start | bytes 1048576 | tf_op jit(solution)/shard_map/all_to_all | solution.py:234
  112.8 2.1 %collective-permute-start.19 = (bf16[256,1024]{1,0:T(8,128)(2,1)S(1)}, bf16[256,1024]{1,0:T(8,128)(2,1)S(1)}, u32[]{:S(2)}, u32[]{:S(2)}) collective-permute-start(bf16[256,1024]{1,0:T(8,128)(2,1)S(1)} %copy-done.8), channel_id=1, source_target_pairs={{0,0},{1,8},{8,1},{9,9},{2,2},{3,10},{10,3},{11,11},{4,4},{5,12},{... | collective-permute-start | bytes 1572872 | tf_op jit(solution)/shard_map/ppermute | solution.py:167
  115.0 2.5 %collective-permute-start.27 = (bf16[512,256]{1,0:T(8,128)(2,1)S(1)}, bf16[512,256]{1,0:T(8,128)(2,1)S(1)}, u32[]{:S(2)}, u32[]{:S(2)}) collective-permute-start(bf16[512,256]{1,0:T(8,128)(2,1)S(1)} %add_convert_fusion.8), channel_id=1, source_target_pairs={{0,32},{32,64},{64,96},{96,128},{128,160},{160,192},{192,224},{224... | collective-permute-start | bytes 786440 | tf_op jit(solution)/shard_map/ppermute | solution.py:171
  117.5 13.9 %collective-permute-done.33 = bf16[512,256]{1,0:T(8,128)(2,1)S(1)} collective-permute-done((bf16[512,256]{1,0:T(8,128)(2,1)S(1)}, bf16[512,256]{1,0:T(8,128)(2,1)S(1)}, u32[]{:S(2)}, u32[]{:S(2)}) %collective-permute-start.33) | collective-permute-done | bytes 262176 | tf_op jit(solution)/shard_map/ppermute | solution.py:171
  132.8 2.7 %collective-permute-start.28 = (bf16[512,256]{1,0:T(8,128)(2,1)S(1)}, bf16[512,256]{1,0:T(8,128)(2,1)S(1)}, u32[]{:S(2)}, u32[]{:S(2)}) collective-permute-start(bf16[512,256]{1,0:T(8,128)(2,1)S(1)} %add_convert_fusion.7), channel_id=1, source_target_pairs={{0,32},{32,64},{64,96},{96,128},{128,160},{160,192},{192,224},{224... | collective-permute-start | bytes 786440 | tf_op jit(solution)/shard_map/ppermute | solution.py:171
  137.0 2.9 %collective-permute-done.34 = bf16[512,256]{1,0:T(8,128)(2,1)S(1)} collective-permute-done((bf16[512,256]{1,0:T(8,128)(2,1)S(1)}, bf16[512,256]{1,0:T(8,128)(2,1)S(1)}, u32[]{:S(2)}, u32[]{:S(2)}) %collective-permute-start.34) | collective-permute-done | bytes 262176 | tf_op jit(solution)/shard_map/ppermute | solution.py:171
  142.8 2.7 %collective-permute-start.29 = (bf16[512,256]{1,0:T(8,128)(2,1)}, bf16[512,256]{1,0:T(8,128)(2,1)S(1)}, u32[]{:S(2)}, u32[]{:S(2)}) collective-permute-start(bf16[512,256]{1,0:T(8,128)(2,1)} %add_convert_fusion.6), channel_id=1, source_target_pairs={{0,32},{32,64},{64,96},{96,128},{128,160},{160,192},{192,224},{224... | collective-permute-start | bytes 786440 | tf_op jit(solution)/shard_map/ppermute | solution.py:171
  145.8 3.9 %collective-permute-start.20 = (bf16[256,1024]{1,0:T(8,128)(2,1)S(1)}, bf16[256,1024]{1,0:T(8,128)(2,1)S(1)}, u32[]{:S(2)}, u32[]{:S(2)}) collective-permute-start(bf16[256,1024]{1,0:T(8,128)(2,1)S(1)} %convolution_convert_fusion), channel_id=1, source_target_pairs={{0,0},{1,8},{8,1},{9,9},{2,2},{3,10},{10,3},{11,11},{4,4},{5,12},{... | collective-permute-start | bytes 1572872 | tf_op jit(solution)/shard_map/ppermute | solution.py:167
  150.7 4.6 %all-to-all-start.3 = ((bf16[8,32,1024]{2,1,0:T(8,128)(2,1)}), bf16[8,32,1024]{2,1,0:T(8,128)(2,1)S(1)}, u32[]{:S(2)}, u32[]{:S(2)}) async-start(bf16[8,32,1024]{2,1,0:T(8,128)(2,1)} %bitcast.14), calls=%async_computation.3 | async-start | bytes 1048576 | tf_op jit(solution)/shard_map/all_to_all | solution.py:236
  155.4 2.2 %collective-permute-start.36 = (bf16[256,256]{1,0:T(8,128)(2,1)S(1)}, bf16[256,256]{1,0:T(8,128)(2,1)S(1)}, u32[]{:S(2)}, u32[]{:S(2)}) collective-permute-start(bf16[256,256]{1,0:T(8,128)(2,1)S(1)} %get-tuple-element.42), channel_id=1, source_target_pairs={{0,0},{1,8},{8,1},{9,9},{2,2},{3,10},{10,3},{11,11},{4,4},{5,12},{... | collective-permute-start | bytes 393224 | tf_op jit(solution)/shard_map/ppermute | solution.py:167
  157.6 3.8 %collective-permute-start.37 = (bf16[256,256]{1,0:T(8,128)(2,1)S(1)}, bf16[256,256]{1,0:T(8,128)(2,1)S(1)}, u32[]{:S(2)}, u32[]{:S(2)}) collective-permute-start(bf16[256,256]{1,0:T(8,128)(2,1)S(1)} %get-tuple-element.43), channel_id=1, source_target_pairs={{0,16},{1,24},{8,17},{9,25},{16,0},{17,8},{24,1},{25,9},{2,18},{3,... | collective-permute-start | bytes 393224 | tf_op jit(solution)/shard_map/ppermute | solution.py:180
  161.4 1.7 collective-permute-done.36
  (147 shorter events, 25.6 us)
Async XLA Ops:
  6.9 24.3 %collective-permute-start = (bf16[256,1024]{1,0:T(8,128)(2,1)}, bf16[256,1024]{1,0:T(8,128)(2,1)S(1)}, u32[]{:S(2)}, u32[]{:S(2)}) collective-permute-start(bf16[256,1024]{1,0:T(8,128)(2,1)} %param.6), channel_id=1, source_target_pairs={{0,0},{1,8},{8,1},{9,9},{2,2},{3,10},{10,3},{11,11},{4,4},{5,12},{... | collective-permute-start | bytes 1572872 | tf_op jit(solution)/shard_map/ppermute | solution.py:167
  16.4 15.9 %all-to-all-start.1 = ((bf16[32,8,1024]{2,0,1:T(8,128)(2,1)}), bf16[32,8,1024]{2,0,1:T(8,128)(2,1)S(1)}, u32[]{:S(2)}, u32[]{:S(2)}) async-start(bf16[32,8,1024]{2,0,1:T(8,128)(2,1)} %bitcast.30), calls=%async_computation.1 | async-start | bytes 1048576 | tf_op jit(solution)/shard_map/all_to_all | solution.py:210
  22.8 18.2 %collective-permute-start.11 = (bf16[512,256]{1,0:T(8,128)(2,1)S(1)}, bf16[512,256]{1,0:T(8,128)(2,1)S(1)}, u32[]{:S(2)}, u32[]{:S(2)}) collective-permute-start(bf16[512,256]{1,0:T(8,128)(2,1)S(1)} %constant_dynamic-update-slice_fusion.2.refs_0_), channel_id=1, source_target_pairs={{0,1},{1,0},{2,3},{3,2},{4,5},{5,4},{6,7},{7,6},{8,9},{9,8},{10,11... | collective-permute-start | bytes 786440 | tf_op jit(solution)/shard_map/ppermute | solution.py:175
  23.5 20.2 %collective-permute-start.18 = (bf16[512,256]{1,0:T(8,128)(2,1)S(1)}, bf16[512,256]{1,0:T(8,128)(2,1)}, u32[]{:S(2)}, u32[]{:S(2)}) collective-permute-start(bf16[512,256]{1,0:T(8,128)(2,1)S(1)} %collective-permute-done.8.refs_7_), channel_id=1, source_target_pairs={{0,1},{1,0},{2,3},{3,2},{4,5},{5,4},{6,7},{7,6},{8,9},{9,8},{10,11... | collective-permute-start | bytes 786440 | tf_op jit(solution)/shard_map/ppermute | solution.py:175
  23.6 17.2 %collective-permute-start.9 = (bf16[512,256]{1,0:T(8,128)(2,1)S(1)}, bf16[512,256]{1,0:T(8,128)(2,1)}, u32[]{:S(2)}, u32[]{:S(2)}) collective-permute-start(bf16[512,256]{1,0:T(8,128)(2,1)S(1)} %collective-permute-done.8.refs_7_), channel_id=1, source_target_pairs={{0,224},{32,0},{64,32},{96,64},{128,96},{160,128},{192,160},{224,1... | collective-permute-start | bytes 786440 | tf_op jit(solution)/shard_map/ppermute | solution.py:171
  28.8 12.5 %collective-permute-start.6 = (bf16[512,256]{1,0:T(8,128)(2,1)S(1)}, bf16[512,256]{1,0:T(8,128)(2,1)}, u32[]{:S(2)}, u32[]{:S(2)}) collective-permute-start(bf16[512,256]{1,0:T(8,128)(2,1)S(1)} %collective-permute-done.5.refs_2_), channel_id=1, source_target_pairs={{0,32},{32,64},{64,96},{96,128},{128,160},{160,192},{192,224},{224... | collective-permute-start | bytes 786440 | tf_op jit(solution)/shard_map/ppermute | solution.py:171
  32.4 30.7 %all-to-all-start = ((bf16[32,8,1024]{2,1,0:T(8,128)(2,1)}), bf16[32,8,1024]{2,1,0:T(8,128)(2,1)S(1)}, u32[]{:S(2)}, u32[]{:S(2)}) async-start(bf16[32,8,1024]{2,1,0:T(8,128)(2,1)} %fusion), calls=%async_computation | async-start | bytes 1048576 | tf_op jit(solution)/shard_map/all_to_all | solution.py:206
  40.9 19.4 %collective-permute-start.10 = (bf16[512,256]{1,0:T(8,128)(2,1)}, bf16[512,256]{1,0:T(8,128)(2,1)}, u32[]{:S(2)}, u32[]{:S(2)}) collective-permute-start(bf16[512,256]{1,0:T(8,128)(2,1)} %collective-permute-done.9.refs_6_), channel_id=1, source_target_pairs={{0,224},{32,0},{64,32},{96,64},{128,96},{160,128},{192,160},{224,1... | collective-permute-start | bytes 786440 | tf_op jit(solution)/shard_map/ppermute | solution.py:171
  41.2 19.9 %collective-permute-start.7 = (bf16[512,256]{1,0:T(8,128)(2,1)}, bf16[512,256]{1,0:T(8,128)(2,1)}, u32[]{:S(2)}, u32[]{:S(2)}) collective-permute-start(bf16[512,256]{1,0:T(8,128)(2,1)} %collective-permute-done.6.refs_3_), channel_id=1, source_target_pairs={{0,32},{32,64},{64,96},{96,128},{128,160},{160,192},{192,224},{224... | collective-permute-start | bytes 786440 | tf_op jit(solution)/shard_map/ppermute | solution.py:171
  43.7 18.1 %collective-permute-start.2 = (bf16[256,1024]{1,0:T(8,128)(2,1)S(1)}, bf16[256,1024]{1,0:T(8,128)(2,1)S(1)}, u32[]{:S(2)}, u32[]{:S(2)}) collective-permute-start(bf16[256,1024]{1,0:T(8,128)(2,1)S(1)} %bitcast.34), channel_id=1, source_target_pairs={{0,0},{1,8},{8,1},{9,9},{2,2},{3,10},{10,3},{11,11},{4,4},{5,12},{... | collective-permute-start | bytes 1572872 | tf_op jit(solution)/shard_map/ppermute | solution.py:167
  46.7 15.0 %collective-permute-start.13 = (bf16[512,256]{1,0:T(8,128)(2,1)S(1)}, bf16[512,256]{1,0:T(8,128)(2,1)S(1)}, u32[]{:S(2)}, u32[]{:S(2)}) collective-permute-start(bf16[512,256]{1,0:T(8,128)(2,1)S(1)} %collective-permute-done.5.refs_2_), channel_id=1, source_target_pairs={{0,1},{1,0},{2,3},{3,2},{4,5},{5,4},{6,7},{7,6},{8,9},{9,8},{10,11... | collective-permute-start | bytes 786440 | tf_op jit(solution)/shard_map/ppermute | solution.py:175
  46.8 15.8 %collective-permute-start.14 = (bf16[512,256]{1,0:T(8,128)(2,1)}, bf16[512,256]{1,0:T(8,128)(2,1)S(1)}, u32[]{:S(2)}, u32[]{:S(2)}) collective-permute-start(bf16[512,256]{1,0:T(8,128)(2,1)} %collective-permute-done.6.refs_3_), channel_id=1, source_target_pairs={{0,1},{1,0},{2,3},{3,2},{4,5},{5,4},{6,7},{7,6},{8,9},{9,8},{10,11... | collective-permute-start | bytes 786440 | tf_op jit(solution)/shard_map/ppermute | solution.py:175
  102.4 12.5 %collective-permute-start.26 = (bf16[512,256]{1,0:T(8,128)(2,1)S(1)}, bf16[512,256]{1,0:T(8,128)(2,1)S(1)}, u32[]{:S(2)}, u32[]{:S(2)}) collective-permute-start(bf16[512,256]{1,0:T(8,128)(2,1)S(1)} %add_convert_fusion.9), channel_id=1, source_target_pairs={{0,32},{32,64},{64,96},{96,128},{128,160},{160,192},{192,224},{224... | collective-permute-start | bytes 786440 | tf_op jit(solution)/shard_map/ppermute | solution.py:171
  102.8 38.0 %all-to-all-start.2 = ((bf16[32,8,1024]{2,1,0:T(8,128)(2,1)}), bf16[32,8,1024]{2,1,0:T(8,128)(2,1)S(1)}, u32[]{:S(2)}, u32[]{:S(2)}) async-start(bf16[32,8,1024]{2,1,0:T(8,128)(2,1)} %bitcast.11), calls=%async_computation.2 | async-start | bytes 1048576 | tf_op jit(solution)/shard_map/all_to_all | solution.py:234
  111.7 19.7 %collective-permute-start.33 = (bf16[512,256]{1,0:T(8,128)(2,1)S(1)}, bf16[512,256]{1,0:T(8,128)(2,1)S(1)}, u32[]{:S(2)}, u32[]{:S(2)}) collective-permute-start(bf16[512,256]{1,0:T(8,128)(2,1)S(1)} %add_convert_fusion.5), channel_id=1, source_target_pairs={{0,224},{32,0},{64,32},{96,64},{128,96},{160,128},{192,160},{224,1... | collective-permute-start | bytes 786440 | tf_op jit(solution)/shard_map/ppermute | solution.py:171
  112.6 19.0 %collective-permute-start.23 = (bf16[512,256]{1,0:T(8,128)(2,1)S(1)}, bf16[512,256]{1,0:T(8,128)(2,1)S(1)}, u32[]{:S(2)}, u32[]{:S(2)}) collective-permute-start(bf16[512,256]{1,0:T(8,128)(2,1)S(1)} %copy-done.17), channel_id=1, source_target_pairs={{0,1},{1,0},{2,3},{3,2},{4,5},{5,4},{6,7},{7,6},{8,9},{9,8},{10,11... | collective-permute-start | bytes 786440 | tf_op jit(solution)/shard_map/ppermute | solution.py:175
  112.8 22.8 %collective-permute-start.19 = (bf16[256,1024]{1,0:T(8,128)(2,1)S(1)}, bf16[256,1024]{1,0:T(8,128)(2,1)S(1)}, u32[]{:S(2)}, u32[]{:S(2)}) collective-permute-start(bf16[256,1024]{1,0:T(8,128)(2,1)S(1)} %copy-done.8), channel_id=1, source_target_pairs={{0,0},{1,8},{8,1},{9,9},{2,2},{3,10},{10,3},{11,11},{4,4},{5,12},{... | collective-permute-start | bytes 1572872 | tf_op jit(solution)/shard_map/ppermute | solution.py:167
  115.0 17.7 %collective-permute-start.27 = (bf16[512,256]{1,0:T(8,128)(2,1)S(1)}, bf16[512,256]{1,0:T(8,128)(2,1)S(1)}, u32[]{:S(2)}, u32[]{:S(2)}) collective-permute-start(bf16[512,256]{1,0:T(8,128)(2,1)S(1)} %add_convert_fusion.8), channel_id=1, source_target_pairs={{0,32},{32,64},{64,96},{96,128},{128,160},{160,192},{192,224},{224... | collective-permute-start | bytes 786440 | tf_op jit(solution)/shard_map/ppermute | solution.py:171
  117.5 19.5 %collective-permute-start.30 = (bf16[512,256]{1,0:T(8,128)(2,1)S(1)}, bf16[512,256]{1,0:T(8,128)(2,1)S(1)}, u32[]{:S(2)}, u32[]{:S(2)}) collective-permute-start(bf16[512,256]{1,0:T(8,128)(2,1)S(1)} %copy-done.14), channel_id=1, source_target_pairs={{0,1},{1,0},{2,3},{3,2},{4,5},{5,4},{6,7},{7,6},{8,9},{9,8},{10,11... | collective-permute-start | bytes 786440 | tf_op jit(solution)/shard_map/ppermute | solution.py:175
  135.5 19.7 %collective-permute-start.21 = (bf16[512,256]{1,0:T(8,128)(2,1)}, bf16[512,256]{1,0:T(8,128)(2,1)S(1)}, u32[]{:S(2)}, u32[]{:S(2)}) collective-permute-start(bf16[512,256]{1,0:T(8,128)(2,1)} %get-tuple-element.25), channel_id=1, source_target_pairs={{0,1},{1,0},{2,3},{3,2},{4,5},{5,4},{6,7},{7,6},{8,9},{9,8},{10,11... | collective-permute-start | bytes 786440 | tf_op jit(solution)/shard_map/ppermute | solution.py:175
  140.7 14.5 %collective-permute-start.35 = (bf16[512,256]{1,0:T(8,128)(2,1)}, bf16[512,256]{1,0:T(8,128)(2,1)S(1)}, u32[]{:S(2)}, u32[]{:S(2)}) collective-permute-start(bf16[512,256]{1,0:T(8,128)(2,1)} %add_convert_fusion.3), channel_id=1, source_target_pairs={{0,224},{32,0},{64,32},{96,64},{128,96},{160,128},{192,160},{224,1... | collective-permute-start | bytes 786440 | tf_op jit(solution)/shard_map/ppermute | solution.py:171
  142.8 12.5 %collective-permute-start.29 = (bf16[512,256]{1,0:T(8,128)(2,1)}, bf16[512,256]{1,0:T(8,128)(2,1)S(1)}, u32[]{:S(2)}, u32[]{:S(2)}) collective-permute-start(bf16[512,256]{1,0:T(8,128)(2,1)} %add_convert_fusion.6), channel_id=1, source_target_pairs={{0,32},{32,64},{64,96},{96,128},{128,160},{160,192},{192,224},{224... | collective-permute-start | bytes 786440 | tf_op jit(solution)/shard_map/ppermute | solution.py:171
  145.8 20.0 %collective-permute-start.20 = (bf16[256,1024]{1,0:T(8,128)(2,1)S(1)}, bf16[256,1024]{1,0:T(8,128)(2,1)S(1)}, u32[]{:S(2)}, u32[]{:S(2)}) collective-permute-start(bf16[256,1024]{1,0:T(8,128)(2,1)S(1)} %convolution_convert_fusion), channel_id=1, source_target_pairs={{0,0},{1,8},{8,1},{9,9},{2,2},{3,10},{10,3},{11,11},{4,4},{5,12},{... | collective-permute-start | bytes 1572872 | tf_op jit(solution)/shard_map/ppermute | solution.py:167
  150.7 14.3 %all-to-all-start.3 = ((bf16[8,32,1024]{2,1,0:T(8,128)(2,1)}), bf16[8,32,1024]{2,1,0:T(8,128)(2,1)S(1)}, u32[]{:S(2)}, u32[]{:S(2)}) async-start(bf16[8,32,1024]{2,1,0:T(8,128)(2,1)} %bitcast.14), calls=%async_computation.3 | async-start | bytes 1048576 | tf_op jit(solution)/shard_map/all_to_all | solution.py:236
  (36 other events, 260.0 us)
